TPU v7x, 512 devices: a whole 4x4x16 slice. The times are simulated.
512 devices in a mesh: dom: 32 (over y, x, core), sub: 16 (over z).
Axes of the slice: x: 4, y: 4, z: 16, core: 2. Of those that a mesh axis runs over, the one named last changes fastest.
Arguments:
- state: float32 [5, 512, 65536], P(None, None, ('dom', 'sub')), may hold values from -1.5 to 7, as said below
- face_links: int32 [3, 3, 65536], P(None, None, ('dom', 'sub')), may hold values from 0 to 703, as said below
- send_from: int32 [512, 320], P(('dom', 'sub')), may hold values from 0 to 384, as said below
Outputs:
- update: float32 [5, 512, 65536], P(None, None, ('dom', 'sub'))
- section: float32 [5, 512, 65536], P(None, None, ('dom', 'sub'))
Inputs may be any that keep to these rules, and one draw needn't show every extreme that they name: `state`: density and pressure are 0.5 or more at every node. face_links[0, k, g]: partner of element g's upper side in direction k, a lower side in direction k: a value below 384 is that lower side's flat index on the same device, a value p from 384 on is received slot p - 384. face_links[1, k, g]: for element g's lower side in direction k, below 384 the flat index of its upper side on the same device, else returned slot minus 3 * 128. face_links[2]: quarter turns, 0 to 3. Every side is in exactly one face. Slots of the blocks for odd dom offsets carry faces in direction 0, of even dom offsets direction 1, of sub offsets direction 2. Two devices share at most 32 faces each way, and in every draw some device shares exactly 32 each way with every neighbour. send_from[d, q] is the flat index of the lower side sent in slot q, or 384 for an empty slot; the first slots of each block are used. The lower side in slot q of block o of device d is the partner of the upper side that the device at offset o links to its slot q of block -o, and that device's slot q of block -o carries a lower side of it in turn.
All inputs are finite; a program needn't handle non-finite values.
Results may differ from a plain program's by a relative error of at most 0.0003.
Values sent between devices are 32-bit elements; how exact they have to be, the bound alone decides.
A program may use at most 128 MiB of HBM per device.

v0:
```python
import jax
import jax.numpy as jnp
import numpy as np
from jax import lax
from jax.sharding import PartitionSpec as P

NP = 8
CAP = 32
W_DOM = 4
SLOTS = 320


GAMMA = 1.4
VISCOSITY = 0.02
CONDUCTION = VISCOSITY * GAMMA / ((GAMMA - 1.0) * 0.72)
PENALTY = 0.4
TIME_STEP = 0.02
SECTION_WEIGHT = 1432997174477.0 / 9575080441755.0


def passed_along(array, axis, by):
    devices = lax.axis_size(axis)
    pairs = [(i, i + by) for i in range(devices) if 0 <= i + by < devices]
    return lax.ppermute(array, axis, pairs)


def lobatto(points):
    poly_order = points - 1
    abscissa = -np.cos(np.pi * np.arange(points) / poly_order)
    for sweep in range(60):
        before = abscissa * 0.0 + 1.0
        current = abscissa
        for degree in range(2, points):
            before, current = (
                current,
                ((2 * degree - 1) * abscissa * current - (degree - 1) * before) / degree,
            )
        abscissa = abscissa - (abscissa * current - before) / (points * current)
    identity = np.eye(points)
    spacing = abscissa[:, None] - abscissa[None, :] + identity
    barycentric = 1.0 / np.prod(spacing, axis=1)
    matrix = barycentric[None, :] / barycentric[:, None] / spacing * (1.0 - identity)
    matrix = matrix - identity * np.sum(matrix, axis=1)[:, None]
    return (matrix, 2.0 / (poly_order * points))


def derivative(matrix, node_field, direction):
    einsum_forms = ("im,cmjle->cijle", "jm,cimle->cijle", "lm,cijme->cijle")
    return jnp.einsum(einsum_forms[direction], matrix, node_field, precision=lax.Precision.HIGHEST)


def face_of(node_field, direction, end_node):
    face_index = (slice(None),) * (direction + 1) + (end_node,)
    return node_field[face_index]


def add_face(node_field, direction, end_node, values):
    face_index = (slice(None),) * (direction + 1) + (end_node,)
    return node_field.at[face_index].add(values)


def lower_traces(state):
    node_cube = state.reshape(5, NP, NP, NP, -1)
    return jnp.concatenate(
        [face_of(node_cube, direction, 0).reshape(5, NP * NP, -1) for direction in range(3)], axis=2
    )


def primitive(conserved):
    density = conserved[0]
    velocity = conserved[1:4] / density
    pressure = (GAMMA - 1.0) * (
        conserved[4]
        - 0.5
        * (conserved[1] * velocity[0] + conserved[2] * velocity[1] + conserved[3] * velocity[2])
    )
    return (density, velocity, pressure)


def euler_flux(conserved, velocity, pressure, direction):
    normal_speed = velocity[direction]
    momentum = conserved[1:4] * normal_speed
    momentum = momentum.at[direction].add(pressure)
    return jnp.concatenate(
        [
            conserved[1 + direction][None],
            momentum,
            ((conserved[4] + pressure) * normal_speed)[None],
        ],
        axis=0,
    )


def viscous_flux(velocity, gradients, direction):
    divergence = gradients[0, 0] + gradients[1, 1] + gradients[2, 2]
    stress = [
        VISCOSITY * (gradients[column, direction] + gradients[direction, column])
        for column in range(3)
    ]
    stress[direction] = stress[direction] - 2.0 / 3.0 * VISCOSITY * divergence
    heat_flux = (
        velocity[0] * stress[0]
        + velocity[1] * stress[1]
        + velocity[2] * stress[2]
        + CONDUCTION * gradients[direction, 3]
    )
    return jnp.stack([jnp.zeros_like(heat_flux)] + stress + [heat_flux], axis=0)


def orient(values, quarter_turns):
    node_grid = values.reshape(values.shape[0], NP, NP, -1)
    result = node_grid
    for quarter in range(1, 4):
        result = jnp.where(
            quarter_turns == quarter, jnp.rot90(node_grid, quarter, axes=(1, 2)), result
        )
    return result.reshape(values.shape)


def element_terms(state, slave_faces, matrix, end_weight):
    node_cube = state.reshape(5, NP, NP, NP, -1)
    elem_count = node_cube.shape[-1]
    density, velocity, pressure = primitive(node_cube)
    lifted = jnp.concatenate([velocity, (pressure / density)[None]], axis=0)
    slave_grid = slave_faces.reshape(5, NP, NP, 3, elem_count)
    slave_density, slave_velocity, slave_pressure = primitive(slave_grid)
    slave_lifted = jnp.concatenate([slave_velocity, (slave_pressure / slave_density)[None]], axis=0)
    gradients = []
    for direction in range(3):
        partial_grad = derivative(matrix, lifted, direction)
        lift_jump = (
            slave_lifted[:, :, :, direction] - face_of(lifted, direction, NP - 1)
        ) / end_weight
        gradients.append(add_face(partial_grad, direction, NP - 1, lift_jump))
    gradients = jnp.stack(gradients)
    sound_speed = jnp.sqrt(GAMMA * pressure / density)
    slave_sound = jnp.sqrt(GAMMA * slave_pressure / slave_density)
    residual_rate = jnp.zeros_like(node_cube)
    master_flux = []
    lower_inner = []
    for direction in range(3):
        euler = euler_flux(node_cube, velocity, pressure, direction)
        viscous = viscous_flux(velocity, gradients, direction)
        total_flux = euler - viscous
        residual_rate = residual_rate - derivative(matrix, total_flux, direction)
        own_face = face_of(node_cube, direction, NP - 1)
        slave_state = slave_grid[:, :, :, direction]
        own_speed = (
            jnp.abs(face_of(velocity, direction, NP - 1)[direction])
            + face_of(sound_speed[None], direction, NP - 1)[0]
        )
        other_speed = (
            jnp.abs(slave_velocity[direction, :, :, direction]) + slave_sound[:, :, direction]
        )
        wave_speed = jnp.maximum(own_speed, other_speed)
        other_euler = euler_flux(
            slave_state,
            slave_velocity[:, :, :, direction],
            slave_pressure[:, :, direction],
            direction,
        )
        numeric = (
            0.5 * (face_of(euler, direction, NP - 1) + other_euler)
            + (0.5 * wave_speed + PENALTY) * (own_face - slave_state)
            - face_of(viscous, direction, NP - 1)
        )
        residual_rate = add_face(
            residual_rate,
            direction,
            NP - 1,
            (face_of(total_flux, direction, NP - 1) - numeric) / end_weight,
        )
        master_flux.append(numeric.reshape(5, NP * NP, elem_count))
        lower_inner.append(face_of(total_flux, direction, 0).reshape(5, NP * NP, elem_count))
    return (
        residual_rate,
        jnp.concatenate(master_flux, axis=2),
        jnp.concatenate(lower_inner, axis=2),
    )


def finish(residual_rate, lower_flux, lower_inner, end_weight):
    elem_count = residual_rate.shape[-1]
    summed = lower_flux + lower_inner
    for direction in range(3):
        one_block = summed[:, :, direction * elem_count : (direction + 1) * elem_count].reshape(
            5, NP, NP, elem_count
        )
        residual_rate = add_face(residual_rate, direction, 0, -one_block / end_weight)
    return residual_rate.reshape(5, NP * NP * NP, elem_count)


def dom_offsets():
    return [offset for offset in range(-W_DOM, W_DOM + 1) if offset != 0]


def split_blocks(buffer):
    return [
        buffer[:, :, block_place * CAP : (block_place + 1) * CAP]
        for block_place in range(2 * W_DOM + 2)
    ]


def pairwise(blocks, move_block):
    offsets = dom_offsets()
    pieces = [None] * len(offsets)
    for block_place, offset in enumerate(offsets):
        pieces[len(offsets) - 1 - block_place] = move_block(blocks[block_place], offset)
    return pieces


def slab_moves(blocks, move_block):
    pieces = [None, None]
    for block_place, offset in enumerate((-1, 1)):
        pieces[1 - block_place] = move_block(blocks[2 * W_DOM + block_place], offset)
    return pieces


def shift_states(one_block, offset):
    return passed_along(one_block, "dom", offset)


def shift_slab_states(one_block, offset):
    return passed_along(one_block, "sub", offset)


def shift_fluxes(one_block, offset):
    return passed_along(one_block, "dom", offset)


def shift_slab_fluxes(one_block, offset):
    return passed_along(one_block, "sub", offset)


def per_device(state, face_links, send_from):
    elem_count = state.shape[2]
    matrix_table, end_weight = lobatto(NP)
    matrix = jnp.asarray(matrix_table, jnp.float32)
    partner = face_links[0].reshape(-1)
    source = face_links[1].reshape(-1)
    quarter_turns = face_links[2].reshape(-1)
    lower = lower_traces(state)
    padded = jnp.concatenate([lower, jnp.zeros((5, NP * NP, 1), lower.dtype)], axis=2)
    outgoing = jnp.take(padded, send_from[0], axis=2)
    state_blocks = split_blocks(outgoing)
    dom_states = pairwise(state_blocks, shift_states)
    inbound = jnp.concatenate(dom_states + slab_moves(state_blocks, shift_slab_states), axis=2)
    gathered = jnp.take(jnp.concatenate([lower, inbound], axis=2), partner, axis=2)
    slave_faces = orient(gathered, quarter_turns)
    residual_rate, master_flux, lower_inner = element_terms(state, slave_faces, matrix, end_weight)
    slave_flux = -orient(master_flux, (4 - quarter_turns) % 4)
    return_slot = jnp.where(partner >= 3 * elem_count, partner - 3 * elem_count, SLOTS)
    returning = (
        jnp.zeros((5, NP * NP, SLOTS), slave_flux.dtype)
        .at[:, :, return_slot]
        .set(slave_flux, mode="drop")
    )
    flux_blocks = split_blocks(returning)
    dom_fluxes = pairwise(flux_blocks, shift_fluxes)
    returned = jnp.concatenate(dom_fluxes + slab_moves(flux_blocks, shift_slab_fluxes), axis=2)
    lower_flux = jnp.take(jnp.concatenate([slave_flux, returned], axis=2), source, axis=2)
    residual_rate = finish(residual_rate, lower_flux, lower_inner, end_weight)
    update = TIME_STEP * residual_rate
    return (update, state + SECTION_WEIGHT * update)


def solution(mesh):
    in_specs = (
        P(None, None, ("dom", "sub")),
        P(None, None, ("dom", "sub")),
        P(("dom", "sub"), None),
    )
    out_specs = (P(None, None, ("dom", "sub")), P(None, None, ("dom", "sub")))
    return jax.shard_map(
        per_device, mesh=mesh, in_specs=in_specs, out_specs=out_specs, check_vma=False
    )
```

profile of v0, /device:TPU:56, one launch (start us, length us, event | category | flops | bytes accessed | tf_op | source)
XLA Modules:
  0.0 245.7 jit_solution(3222007360840931758)
XLA Ops:
  6.7 2.4 gather_fusion
  9.1 2.2 select_bitcast_fusion.1
  12.3 4.9 %collective-permute-start = (f32[5,64,32]{1,0,2:T(8,128)}, f32[5,64,32]{1,0,2:T(8,128)}, u32[]{:S(2)}, u32[]{:S(2)}) collective-permute-start(f32[5,64,32]{1,0,2:T(8,128)} %get-tuple-element.245), channel_id=1, source_target_pairs={{0,64},{16,80},{32,96},{48,112},{64,128},{80,144},{96,160},{112,17... | collective-permute-start | bytes 122888 | tf_op jit(solution)/shard_map/ppermute | solution.py:24
  17.3 1.9 collective-permute-start.1
  19.2 2.5 %collective-permute-start.2 = (f32[5,64,32]{1,0,2:T(8,128)}, f32[5,64,32]{1,0,2:T(8,128)}, u32[]{:S(2)}, u32[]{:S(2)}) collective-permute-start(f32[5,64,32]{1,0,2:T(8,128)} %get-tuple-element.243), channel_id=1, source_target_pairs={{0,32},{16,48},{32,64},{48,80},{64,96},{80,112},{96,128},{112,144}... | collective-permute-start | bytes 122888 | tf_op jit(solution)/shard_map/ppermute | solution.py:24
  21.7 1.9 collective-permute-start.3
  23.6 5.9 %collective-permute-start.4 = (f32[5,64,32]{1,0,2:T(8,128)}, f32[5,64,32]{1,0,2:T(8,128)}, u32[]{:S(2)}, u32[]{:S(2)}) collective-permute-start(f32[5,64,32]{1,0,2:T(8,128)} %get-tuple-element.241), channel_id=1, source_target_pairs={{16,0},{32,16},{48,32},{64,48},{80,64},{96,80},{112,96},{128,112},... | collective-permute-start | bytes 122888 | tf_op jit(solution)/shard_map/ppermute | solution.py:24
  39.7 2.2 multiply_bitcast_fusion
  61.4 3.3 %collective-permute-start.5 = (f32[5,64,32]{1,0,2:T(8,128)S(1)}, f32[5,64,32]{1,0,2:T(8,128)S(1)}, u32[]{:S(2)}, u32[]{:S(2)}) collective-permute-start(f32[5,64,32]{1,0,2:T(8,128)S(1)} %copy-done.90), channel_id=1, source_target_pairs={{32,0},{48,16},{64,32},{80,48},{96,64},{112,80},{128,96},{144,112}... | collective-permute-start | bytes 122888 | tf_op jit(solution)/shard_map/ppermute | solution.py:24
  66.3 2.2 collective-permute-start.6
  70.1 4.4 %collective-permute-start.7 = (f32[5,64,32]{1,0,2:T(8,128)S(1)}, f32[5,64,32]{1,0,2:T(8,128)S(1)}, u32[]{:S(2)}, u32[]{:S(2)}) collective-permute-start(f32[5,64,32]{1,0,2:T(8,128)S(1)} %copy-done.88), channel_id=1, source_target_pairs={{64,0},{80,16},{96,32},{112,48},{128,64},{144,80},{160,96},{176,11... | collective-permute-start | bytes 122888 | tf_op jit(solution)/shard_map/ppermute | solution.py:24
  76.1 3.8 %collective-permute-start.8 = (f32[5,64,32]{1,0,2:T(8,128)S(1)}, f32[5,64,32]{1,0,2:T(8,128)S(1)}, u32[]{:S(2)}, u32[]{:S(2)}) collective-permute-start(f32[5,64,32]{1,0,2:T(8,128)S(1)} %copy-done.87), channel_id=1, source_target_pairs={{0,1},{1,2},{2,3},{3,4},{4,5},{5,6},{6,7},{7,8},{8,9},{9,10},{10,1... | collective-permute-start | bytes 122888 | tf_op jit(solution)/shard_map/ppermute | solution.py:24
  81.5 2.2 collective-permute-start.9
  89.5 3.9 %gather_fusion.1 = f32[384,5,64]{2,1,0:T(8,128)} fusion(f32[5,64,704]{1,0,2:T(8,128)} %constant_dynamic-update-slice_fusion, s32[1024]{0:T(1024)S(1)} %pad_clamp_fusion.1), kind=kCustom, calls=%fused_computation.clone | custom fusion | bytes 984576 | tf_op jit(solution)/shard_map/jit(_take)/gather | solution.py:248
  93.4 3.1 %select_bitcast_fusion = f32[5,64,384]{1,0,2:T(8,128)} fusion(f32[384,5,64]{2,1,0:T(8,128)} %gather_fusion.1, pred[384]{0:T(512)(128)(4,1)} %get-tuple-element.314), kind=kLoop, calls=%fused_computation.7 | loop fusion | flops 122880 | bytes 983424 | tf_op jit(solution)/shard_map/jit(_take)/select_n | solution.py:248
  109.0 3.3 %scatter-add.51 = f32[1,4,8,8,8,128]{5,2,3,4,1,0:T(8,128)S(1)} dynamic-update-slice(f32[1,4,8,8,8,128]{5,2,3,4,1,0:T(8,128)S(1)} %bitcast.521, f32[1,4,1,8,8,128]{5,2,3,4,1,0:T(1,128)} %bitcast.549, s32[]{:T(128)} %constant.454.clone.1, s32[]{:T(128)} %constant.454.clone.1, s32[]{:T(128)} %constant.462.clone.1, s32[]{:T(128)} %constant.454.clone.1, s32[]{:T(128)} %constant.454.clone.1, ...) | dynamic-update-slice | bytes 262148 | tf_op jit(solution)/shard_map/scatter-add | solution.py:59
  122.3 2.4 fusion.3
  139.3 5.5 %scatter-add.59 = f32[5,8,8,8,128]{4,1,2,3,0:T(8,128)} dynamic-update-slice(f32[5,8,8,8,128]{4,1,2,3,0:T(8,128)} %copy-done.6, f32[5,1,8,8,128]{4,1,2,3,0:T(1,128)} %get-tuple-element.212, s32[]{:T(128)} %constant.454.clone.1, s32[]{:T(128)} %constant.462.clone.1, s32[]{:T(128)} %constant.454.clone.1, s32[]{:T(128)} %constant.454.clone.1, s32[]{:T(128)} %constant.454.clone.1) | dynamic-update-slice | bytes 327684 | tf_op jit(solution)/shard_map/scatter-add | solution.py:59
  144.7 2.5 %bitcast_subtract_fusion.1 = f32[5,8,8,8,128]{4,1,2,3,0:T(8,128)S(1)} fusion(f32[5,8,8,8,128]{4,1,2,3,0:T(8,128)} %scatter-add.59, f32[5,8,8,128,8]{3,4,2,1,0:T(8,128)} %fusion.3), kind=kLoop, calls=%fused_computation.15 | loop fusion | flops 327680 | bytes 3932160 | tf_op jit(solution)/shard_map/sub | solution.py:145
  148.8 3.1 %fusion.1 = f32[5,8,8,128,8]{3,4,2,1,0:T(8,128)} fusion(f32[8,8,1,1,1]{1,0,4,3,2:T(8,128)S(1)} %copy-done.98, f32[5,8,8,8,128]{4,1,2,0,3:T(8,128)S(1)} %get-tuple-element.222), kind=kOutput, calls=%fused_computation.16 | convolution fusion | flops 31457280 | bytes 2621696 | tf_op jit(solution)/shard_map/lm,cijme->cijle/dot_general | solution.py:49
  157.5 23.0 %scatter_fusion = f32[5,64,320]{1,0,2:T(8,128)S(1)} fusion(f32[5,64,320]{1,0,2:T(8,128)S(1)} %broadcast_in_dim.78, s32[384]{0:T(512)S(1)} %fusion.125, f32[384,5,64]{2,1,0:T(8,128)} %copy.683), kind=kCustom, calls=%fused_computation.3 | custom fusion | bytes 1476096 | tf_op jit(solution)/shard_map/scatter | solution.py:256
  180.7 3.1 %collective-permute-start.10 = (f32[5,64,32]{1,0,2:T(8,128)S(1)}, f32[5,64,32]{1,0,2:T(8,128)S(1)}, u32[]{:S(2)}, u32[]{:S(2)}) collective-permute-start(f32[5,64,32]{1,0,2:T(8,128)S(1)} %get-tuple-element.210), channel_id=1, source_target_pairs={{0,64},{16,80},{32,96},{48,112},{64,128},{80,144},{96,160},{112,17... | collective-permute-start | bytes 122888 | tf_op jit(solution)/shard_map/ppermute | solution.py:24
  191.7 2.3 collective-permute-start.12
  194.0 1.9 collective-permute-start.13
  195.9 5.8 %collective-permute-start.14 = (f32[5,64,32]{1,0,2:T(8,128)S(1)}, f32[5,64,32]{1,0,2:T(8,128)S(1)}, u32[]{:S(2)}, u32[]{:S(2)}) collective-permute-start(f32[5,64,32]{1,0,2:T(8,128)S(1)} %get-tuple-element.206), channel_id=1, source_target_pairs={{16,0},{32,16},{48,32},{64,48},{80,64},{96,80},{112,96},{128,112},... | collective-permute-start | bytes 122888 | tf_op jit(solution)/shard_map/ppermute | solution.py:24
  201.7 3.6 %collective-permute-start.15 = (f32[5,64,32]{1,0,2:T(8,128)S(1)}, f32[5,64,32]{1,0,2:T(8,128)S(1)}, u32[]{:S(2)}, u32[]{:S(2)}) collective-permute-start(f32[5,64,32]{1,0,2:T(8,128)S(1)} %get-tuple-element.205), channel_id=1, source_target_pairs={{32,0},{48,16},{64,32},{80,48},{96,64},{112,80},{128,96},{144,112}... | collective-permute-start | bytes 122888 | tf_op jit(solution)/shard_map/ppermute | solution.py:24
  205.9 2.1 collective-permute-start.16
  208.8 6.6 %collective-permute-start.17 = (f32[5,64,32]{1,0,2:T(8,128)S(1)}, f32[5,64,32]{1,0,2:T(8,128)S(1)}, u32[]{:S(2)}, u32[]{:S(2)}) collective-permute-start(f32[5,64,32]{1,0,2:T(8,128)S(1)} %get-tuple-element.203), channel_id=1, source_target_pairs={{64,0},{80,16},{96,32},{112,48},{128,64},{144,80},{160,96},{176,11... | collective-permute-start | bytes 122888 | tf_op jit(solution)/shard_map/ppermute | solution.py:24
  216.0 5.3 %collective-permute-start.18 = (f32[5,64,32]{1,0,2:T(8,128)S(1)}, f32[5,64,32]{1,0,2:T(8,128)S(1)}, u32[]{:S(2)}, u32[]{:S(2)}) collective-permute-start(f32[5,64,32]{1,0,2:T(8,128)S(1)} %get-tuple-element.202), channel_id=1, source_target_pairs={{0,1},{1,2},{2,3},{3,4},{4,5},{5,6},{6,7},{7,8},{8,9},{9,10},{10,1... | collective-permute-start | bytes 122888 | tf_op jit(solution)/shard_map/ppermute | solution.py:24
  227.2 3.6 %collective-permute-done.19 = f32[5,64,32]{1,0,2:T(8,128)S(1)} collective-permute-done((f32[5,64,32]{1,0,2:T(8,128)S(1)}, f32[5,64,32]{1,0,2:T(8,128)S(1)}, u32[]{:S(2)}, u32[]{:S(2)}) %collective-permute-start.19) | collective-permute-done | bytes 40992 | tf_op jit(solution)/shard_map/ppermute | solution.py:24
  231.4 3.9 %gather_fusion.2 = f32[384,5,64]{2,1,0:T(8,128)} fusion(f32[5,64,704]{1,0,2:T(8,128)} %constant_dynamic-update-slice_fusion.15, s32[1024]{0:T(1024)S(1)} %pad_clamp_fusion), kind=kCustom, calls=%fused_computation.1.clone | custom fusion | bytes 984576 | tf_op jit(solution)/shard_map/jit(_take)/gather | solution.py:261
  238.3 3.2 %scatter-add.70 = f32[5,8,8,8,128]{4,1,2,0,3:T(8,128)S(1)} dynamic-update-slice(f32[5,8,8,8,128]{4,1,2,0,3:T(8,128)S(1)} %get-tuple-element.218, f32[5,1,8,8,128]{4,1,2,0,3:T(1,128)S(1)} %slice_add_fusion.8, s32[]{:T(128)} %constant.454.clone.1, s32[]{:T(128)} %constant.454.clone.1, s32[]{:T(128)} %constant.454.clone.1, s32[]{:T(128)} %constant.454.clone.1, s32[]{:T(128)} %constant.454.clone.1) | dynamic-update-slice | bytes 327684 | tf_op jit(solution)/shard_map/scatter-add | solution.py:59
  (382 shorter events, 115.4 us)
Async XLA Ops:
  12.3 49.0 %collective-permute-start = (f32[5,64,32]{1,0,2:T(8,128)}, f32[5,64,32]{1,0,2:T(8,128)}, u32[]{:S(2)}, u32[]{:S(2)}) collective-permute-start(f32[5,64,32]{1,0,2:T(8,128)} %get-tuple-element.245), channel_id=1, source_target_pairs={{0,64},{16,80},{32,96},{48,112},{64,128},{80,144},{96,160},{112,17... | collective-permute-start | bytes 122888 | tf_op jit(solution)/shard_map/ppermute | solution.py:24
  17.3 49.0 %collective-permute-start.1 = (f32[5,64,32]{1,0,2:T(8,128)}, f32[5,64,32]{1,0,2:T(8,128)}, u32[]{:S(2)}, u32[]{:S(2)}) collective-permute-start(f32[5,64,32]{1,0,2:T(8,128)} %get-tuple-element.244), channel_id=1, source_target_pairs={{0,48},{16,64},{32,80},{48,96},{64,112},{80,128},{96,144},{112,160... | collective-permute-start | bytes 122888 | tf_op jit(solution)/shard_map/ppermute | solution.py:24
  19.2 50.9 %collective-permute-start.2 = (f32[5,64,32]{1,0,2:T(8,128)}, f32[5,64,32]{1,0,2:T(8,128)}, u32[]{:S(2)}, u32[]{:S(2)}) collective-permute-start(f32[5,64,32]{1,0,2:T(8,128)} %get-tuple-element.243), channel_id=1, source_target_pairs={{0,32},{16,48},{32,64},{48,80},{64,96},{80,112},{96,128},{112,144}... | collective-permute-start | bytes 122888 | tf_op jit(solution)/shard_map/ppermute | solution.py:24
  21.7 54.4 %collective-permute-start.3 = (f32[5,64,32]{1,0,2:T(8,128)}, f32[5,64,32]{1,0,2:T(8,128)}, u32[]{:S(2)}, u32[]{:S(2)}) collective-permute-start(f32[5,64,32]{1,0,2:T(8,128)} %get-tuple-element.242), channel_id=1, source_target_pairs={{0,16},{16,32},{32,48},{48,64},{64,80},{80,96},{96,112},{112,128},... | collective-permute-start | bytes 122888 | tf_op jit(solution)/shard_map/ppermute | solution.py:24
  23.6 57.8 %collective-permute-start.4 = (f32[5,64,32]{1,0,2:T(8,128)}, f32[5,64,32]{1,0,2:T(8,128)}, u32[]{:S(2)}, u32[]{:S(2)}) collective-permute-start(f32[5,64,32]{1,0,2:T(8,128)} %get-tuple-element.241), channel_id=1, source_target_pairs={{16,0},{32,16},{48,32},{64,48},{80,64},{96,80},{112,96},{128,112},... | collective-permute-start | bytes 122888 | tf_op jit(solution)/shard_map/ppermute | solution.py:24
  30.5 5.1 %copy-start.25 = (f32[1,512,128]{2,1,0:T(8,128)}, f32[1,512,128]{2,1,0:T(8,128)S(1)}, u32[]{:S(2)}) copy-start(f32[1,512,128]{2,1,0:T(8,128)S(1)} %get-tuple-element.249) | copy-start | bytes 786436
  30.5 6.2 %copy-start.24 = (f32[1,512,128]{2,1,0:T(8,128)}, f32[1,512,128]{2,1,0:T(8,128)S(1)}, u32[]{:S(2)}) copy-start(f32[1,512,128]{2,1,0:T(8,128)S(1)} %get-tuple-element.246) | copy-start | bytes 786436
  41.9 7.5 %copy-start.70 = (f32[1,8,8,8,128]{4,1,2,3,0:T(8,128)}, f32[1,8,8,8,128]{4,1,2,3,0:T(8,128)S(1)}, u32[]{:S(2)}) copy-start(f32[1,8,8,8,128]{4,1,2,3,0:T(8,128)S(1)} %get-tuple-element.299) | copy-start | bytes 786436
  58.3 8.0 %copy-start.89 = (f32[5,64,32]{1,0,2:T(8,128)S(1)}, f32[5,64,32]{1,0,2:T(8,128)}, u32[]{:S(2)}) copy-start(f32[5,64,32]{1,0,2:T(8,128)} %get-tuple-element.239) | copy-start | bytes 122884
  58.3 11.8 %copy-start.88 = (f32[5,64,32]{1,0,2:T(8,128)S(1)}, f32[5,64,32]{1,0,2:T(8,128)}, u32[]{:S(2)}) copy-start(f32[5,64,32]{1,0,2:T(8,128)} %get-tuple-element.238) | copy-start | bytes 122884
  58.3 17.8 %copy-start.87 = (f32[5,64,32]{1,0,2:T(8,128)S(1)}, f32[5,64,32]{1,0,2:T(8,128)}, u32[]{:S(2)}) copy-start(f32[5,64,32]{1,0,2:T(8,128)} %get-tuple-element.237) | copy-start | bytes 122884
  61.4 23.9 %collective-permute-start.5 = (f32[5,64,32]{1,0,2:T(8,128)S(1)}, f32[5,64,32]{1,0,2:T(8,128)S(1)}, u32[]{:S(2)}, u32[]{:S(2)}) collective-permute-start(f32[5,64,32]{1,0,2:T(8,128)S(1)} %copy-done.90), channel_id=1, source_target_pairs={{32,0},{48,16},{64,32},{80,48},{96,64},{112,80},{128,96},{144,112}... | collective-permute-start | bytes 122888 | tf_op jit(solution)/shard_map/ppermute | solution.py:24
  66.3 19.7 %collective-permute-start.6 = (f32[5,64,32]{1,0,2:T(8,128)S(1)}, f32[5,64,32]{1,0,2:T(8,128)S(1)}, u32[]{:S(2)}, u32[]{:S(2)}) collective-permute-start(f32[5,64,32]{1,0,2:T(8,128)S(1)} %copy-done.89), channel_id=1, source_target_pairs={{48,0},{64,16},{80,32},{96,48},{112,64},{128,80},{144,96},{160,112... | collective-permute-start | bytes 122888 | tf_op jit(solution)/shard_map/ppermute | solution.py:24
  70.1 16.5 %collective-permute-start.7 = (f32[5,64,32]{1,0,2:T(8,128)S(1)}, f32[5,64,32]{1,0,2:T(8,128)S(1)}, u32[]{:S(2)}, u32[]{:S(2)}) collective-permute-start(f32[5,64,32]{1,0,2:T(8,128)S(1)} %copy-done.88), channel_id=1, source_target_pairs={{64,0},{80,16},{96,32},{112,48},{128,64},{144,80},{160,96},{176,11... | collective-permute-start | bytes 122888 | tf_op jit(solution)/shard_map/ppermute | solution.py:24
  76.1 11.2 %collective-permute-start.8 = (f32[5,64,32]{1,0,2:T(8,128)S(1)}, f32[5,64,32]{1,0,2:T(8,128)S(1)}, u32[]{:S(2)}, u32[]{:S(2)}) collective-permute-start(f32[5,64,32]{1,0,2:T(8,128)S(1)} %copy-done.87), channel_id=1, source_target_pairs={{0,1},{1,2},{2,3},{3,4},{4,5},{5,6},{6,7},{7,8},{8,9},{9,10},{10,1... | collective-permute-start | bytes 122888 | tf_op jit(solution)/shard_map/ppermute | solution.py:24
  81.5 7.4 %collective-permute-start.9 = (f32[5,64,32]{1,0,2:T(8,128)S(1)}, f32[5,64,32]{1,0,2:T(8,128)S(1)}, u32[]{:S(2)}, u32[]{:S(2)}) collective-permute-start(f32[5,64,32]{1,0,2:T(8,128)S(1)} %get-tuple-element.236), channel_id=1, source_target_pairs={{1,0},{2,1},{3,2},{4,3},{5,4},{6,5},{7,6},{8,7},{9,8},{10,9},{11,1... | collective-permute-start | bytes 122888 | tf_op jit(solution)/shard_map/ppermute | solution.py:24
  104.8 22.1 %copy-start.80 = (f32[1,8,8,1,128]{4,2,3,1,0:T(8,128)}, f32[1,8,8,1,128]{4,2,3,1,0:T(8,128)S(1)}, u32[]{:S(2)}) copy-start(f32[1,8,8,1,128]{4,2,3,1,0:T(8,128)S(1)} %get-tuple-element.273) | copy-start | bytes 98308
  119.5 14.9 %copy-start.23 = (f32[5,8,8,8,128]{4,1,2,3,0:T(8,128)}, f32[5,8,8,8,128]{4,1,2,3,0:T(8,128)S(1)}, u32[]{:S(2)}) copy-start(f32[5,8,8,8,128]{4,1,2,3,0:T(8,128)S(1)} %get-tuple-element.230) | copy-start | bytes 3932164
  122.3 12.1 %copy-start.31 = (f32[5,8,8,8,128]{4,1,2,3,0:T(8,128)}, f32[5,8,8,8,128]{4,1,2,3,0:T(8,128)S(1)}, u32[]{:S(2)}) copy-start(f32[5,8,8,8,128]{4,1,2,3,0:T(8,128)S(1)} %get-tuple-element.325) | copy-start | bytes 3932164
  125.7 8.5 %copy-start.21 = (f32[5,8,8,8,128]{4,1,2,0,3:T(8,128)}, f32[5,8,8,8,128]{4,1,2,0,3:T(8,128)S(1)}, u32[]{:S(2)}) copy-start(f32[5,8,8,8,128]{4,1,2,0,3:T(8,128)S(1)} %fusion.16) | copy-start | bytes 3932164
  131.9 16.9 %copy-start.2 = (f32[5,8,8,8,128]{4,1,2,0,3:T(8,128)}, f32[5,8,8,8,128]{4,1,2,0,3:T(8,128)S(1)}, u32[]{:S(2)}) copy-start(f32[5,8,8,8,128]{4,1,2,0,3:T(8,128)S(1)} %get-tuple-element.222) | copy-start | bytes 3932164
  180.7 21.0 %collective-permute-start.10 = (f32[5,64,32]{1,0,2:T(8,128)S(1)}, f32[5,64,32]{1,0,2:T(8,128)S(1)}, u32[]{:S(2)}, u32[]{:S(2)}) collective-permute-start(f32[5,64,32]{1,0,2:T(8,128)S(1)} %get-tuple-element.210), channel_id=1, source_target_pairs={{0,64},{16,80},{32,96},{48,112},{64,128},{80,144},{96,160},{112,17... | collective-permute-start | bytes 122888 | tf_op jit(solution)/shard_map/ppermute | solution.py:24
  189.8 16.1 %collective-permute-start.11 = (f32[5,64,32]{1,0,2:T(8,128)S(1)}, f32[5,64,32]{1,0,2:T(8,128)S(1)}, u32[]{:S(2)}, u32[]{:S(2)}) collective-permute-start(f32[5,64,32]{1,0,2:T(8,128)S(1)} %get-tuple-element.209), channel_id=1, source_target_pairs={{0,48},{16,64},{32,80},{48,96},{64,112},{80,128},{96,144},{112,160... | collective-permute-start | bytes 122888 | tf_op jit(solution)/shard_map/ppermute | solution.py:24
  191.7 17.0 %collective-permute-start.12 = (f32[5,64,32]{1,0,2:T(8,128)S(1)}, f32[5,64,32]{1,0,2:T(8,128)S(1)}, u32[]{:S(2)}, u32[]{:S(2)}) collective-permute-start(f32[5,64,32]{1,0,2:T(8,128)S(1)} %get-tuple-element.208), channel_id=1, source_target_pairs={{0,32},{16,48},{32,64},{48,80},{64,96},{80,112},{96,128},{112,144}... | collective-permute-start | bytes 122888 | tf_op jit(solution)/shard_map/ppermute | solution.py:24
  194.0 22.0 %collective-permute-start.13 = (f32[5,64,32]{1,0,2:T(8,128)S(1)}, f32[5,64,32]{1,0,2:T(8,128)S(1)}, u32[]{:S(2)}, u32[]{:S(2)}) collective-permute-start(f32[5,64,32]{1,0,2:T(8,128)S(1)} %get-tuple-element.207), channel_id=1, source_target_pairs={{0,16},{16,32},{32,48},{48,64},{64,80},{80,96},{96,112},{112,128},... | collective-permute-start | bytes 122888 | tf_op jit(solution)/shard_map/ppermute | solution.py:24
  195.9 26.0 %collective-permute-start.14 = (f32[5,64,32]{1,0,2:T(8,128)S(1)}, f32[5,64,32]{1,0,2:T(8,128)S(1)}, u32[]{:S(2)}, u32[]{:S(2)}) collective-permute-start(f32[5,64,32]{1,0,2:T(8,128)S(1)} %get-tuple-element.206), channel_id=1, source_target_pairs={{16,0},{32,16},{48,32},{64,48},{80,64},{96,80},{112,96},{128,112},... | collective-permute-start | bytes 122888 | tf_op jit(solution)/shard_map/ppermute | solution.py:24
  201.7 22.8 %collective-permute-start.15 = (f32[5,64,32]{1,0,2:T(8,128)S(1)}, f32[5,64,32]{1,0,2:T(8,128)S(1)}, u32[]{:S(2)}, u32[]{:S(2)}) collective-permute-start(f32[5,64,32]{1,0,2:T(8,128)S(1)} %get-tuple-element.205), channel_id=1, source_target_pairs={{32,0},{48,16},{64,32},{80,48},{96,64},{112,80},{128,96},{144,112}... | collective-permute-start | bytes 122888 | tf_op jit(solution)/shard_map/ppermute | solution.py:24
  205.9 19.2 %collective-permute-start.16 = (f32[5,64,32]{1,0,2:T(8,128)S(1)}, f32[5,64,32]{1,0,2:T(8,128)S(1)}, u32[]{:S(2)}, u32[]{:S(2)}) collective-permute-start(f32[5,64,32]{1,0,2:T(8,128)S(1)} %get-tuple-element.204), channel_id=1, source_target_pairs={{48,0},{64,16},{80,32},{96,48},{112,64},{128,80},{144,96},{160,112... | collective-permute-start | bytes 122888 | tf_op jit(solution)/shard_map/ppermute | solution.py:24
  208.8 17.1 %collective-permute-start.17 = (f32[5,64,32]{1,0,2:T(8,128)S(1)}, f32[5,64,32]{1,0,2:T(8,128)S(1)}, u32[]{:S(2)}, u32[]{:S(2)}) collective-permute-start(f32[5,64,32]{1,0,2:T(8,128)S(1)} %get-tuple-element.203), channel_id=1, source_target_pairs={{64,0},{80,16},{96,32},{112,48},{128,64},{144,80},{160,96},{176,11... | collective-permute-start | bytes 122888 | tf_op jit(solution)/shard_map/ppermute | solution.py:24
  216.0 10.5 %collective-permute-start.18 = (f32[5,64,32]{1,0,2:T(8,128)S(1)}, f32[5,64,32]{1,0,2:T(8,128)S(1)}, u32[]{:S(2)}, u32[]{:S(2)}) collective-permute-start(f32[5,64,32]{1,0,2:T(8,128)S(1)} %get-tuple-element.202), channel_id=1, source_target_pairs={{0,1},{1,2},{2,3},{3,4},{4,5},{5,6},{6,7},{7,8},{8,9},{9,10},{10,1... | collective-permute-start | bytes 122888 | tf_op jit(solution)/shard_map/ppermute | solution.py:24
  221.9 8.8 %collective-permute-start.19 = (f32[5,64,32]{1,0,2:T(8,128)S(1)}, f32[5,64,32]{1,0,2:T(8,128)S(1)}, u32[]{:S(2)}, u32[]{:S(2)}) collective-permute-start(f32[5,64,32]{1,0,2:T(8,128)S(1)} %get-tuple-element.201), channel_id=1, source_target_pairs={{1,0},{2,1},{3,2},{4,3},{5,4},{6,5},{7,6},{8,7},{9,8},{10,9},{11,1... | collective-permute-start | bytes 122888 | tf_op jit(solution)/shard_map/ppermute | solution.py:24
  231.4 5.6 %copy-start.102 = (pred[384]{0:T(512)(128)(4,1)S(1)}, pred[384]{0:T(512)(128)(4,1)}, u32[]{:S(2)}) copy-start(pred[384]{0:T(512)(128)(4,1)} %get-tuple-element.313) | copy-start | bytes 1156
  (95 other events, 203.6 us)
where the time goes:
time: 249 us; the launch traced here: 246 us
  local copies, waits for them, and re-layouts  121 us (49%)
  starting transfers between devices  67.6 us (27%)
  other arithmetic  40.3 us (16%)
  matrix products  10.4 us (4%)
  waiting for transfers between devices  4.51 us (2%)
    ppermute x20, starting transfers between devices, passed_along(): return lax.ppermute(array, axis, pairs)  67.6 us
    unnamed x245, local copies, waits for them, and re-layouts  34.3 us
    scatter x1, local copies, waits for them, and re-layouts, per_device(): returning = jnp.zeros((5, NP * NP, SLOTS), slave_flux.dtype).at[:, :, ret...  23 us
    scatter-add x3, local copies, waits for them, and re-layouts, add_face(): return node_field.at[face_index].add(values)  12 us
    dot_general x6, matrix products, derivative(): jnp.einsum(einsum_forms[direction], matrix, node_field, precision=lax.Pre...  10.4 us
    slice x7, local copies, waits for them, and re-layouts, face_of(): return node_field[face_index]  6 us
    gather x2, local copies, waits for them, and re-layouts, per_device(): jnp.take(jnp.concatenate([slave_flux, returned], axis=2), source, axis=2)  5.61 us
    unnamed x7, other arithmetic  5.38 us
  transfers between devices with their start and end apart: 20, of which 2 were waited for; matrix products, arithmetic and copies ran while one was open for 21% of the time, Pallas kernels for 0%

commit v1 on v0

v1 whole, which is shorter than its diff:
```python
import functools

import jax
import jax.numpy as jnp
import numpy as np
from jax import lax
from jax.experimental import pallas as pl
from jax.experimental.pallas import tpu as pltpu
from jax.sharding import PartitionSpec as P

NP = 8
LANES = 128
GAMMA = 1.4
VISCOSITY = 0.02
CONDUCTION = VISCOSITY * GAMMA / ((GAMMA - 1.0) * 0.72)
PENALTY = 0.4
TIME_STEP = 0.02
SECTION_WEIGHT = 1432997174477.0 / 9575080441755.0
OFFSETS = [("dom", o) for o in (-4, -3, -2, -1, 1, 2, 3, 4)] + [("sub", -1), ("sub", 1)]
MIRROR = [7, 6, 5, 4, 3, 2, 1, 0, 9, 8]
PLACES = [[1, 3, 4, 6], [0, 2, 5, 7], [8, 9]]


def lobatto(points):
    poly_order = points - 1
    abscissa = -np.cos(np.pi * np.arange(points) / poly_order)
    for sweep in range(60):
        before = abscissa * 0.0 + 1.0
        current = abscissa
        for degree in range(2, points):
            before, current = (
                current,
                ((2 * degree - 1) * abscissa * current - (degree - 1) * before) / degree,
            )
        abscissa = abscissa - (abscissa * current - before) / (points * current)
    identity = np.eye(points)
    spacing = abscissa[:, None] - abscissa[None, :] + identity
    barycentric = 1.0 / np.prod(spacing, axis=1)
    matrix = barycentric[None, :] / barycentric[:, None] / spacing * (1.0 - identity)
    matrix = matrix - identity * np.sum(matrix, axis=1)[:, None]
    return (matrix, 2.0 / (poly_order * points))


DMAT, W_END = lobatto(NP)
GRAD_MAT = VISCOSITY * DMAT
LIFT = VISCOSITY / W_END
FLUX_MAT = DMAT.copy()
FLUX_MAT[NP - 1, NP - 1] -= 1.0 / W_END
FLUX_MAT[0, 0] += 1.0 / W_END
FLUX_MAT = -TIME_STEP * FLUX_MAT
FACE_SCALE = TIME_STEP / W_END


def iota(axis):
    return lax.broadcasted_iota(jnp.int32, (NP, LANES), axis)


def lane_gather(x, index):
    return jnp.take_along_axis(x, index, axis=1, mode="promise_in_bounds")


def row_gather(x, index):
    return jnp.take_along_axis(x, index, axis=0, mode="promise_in_bounds")


def pencil(matrix, xs):
    even = [xs[m] + xs[7 - m] for m in range(4)]
    odd = [xs[m] - xs[7 - m] for m in range(4)]
    out = [None] * 8
    for i in range(4):
        a = b = None
        for m in range(4):
            ce = float(0.5 * (matrix[i, m] + matrix[i, 7 - m]))
            co = float(0.5 * (matrix[i, m] - matrix[i, 7 - m]))
            a = ce * even[m] if a is None else a + ce * even[m]
            b = co * odd[m] if b is None else b + co * odd[m]
        out[i] = a + b
        out[7 - i] = b - a
    return out


def roll_table(matrix):
    row = iota(0)
    table = []
    for r in range(NP):
        c = jnp.zeros((NP, LANES), jnp.float32)
        for l in range(NP):
            c = jnp.where(row == l, float(matrix[l, (l - r) % NP]), c)
        table.append(c)
    return table


def along_rows(table, x):
    acc = table[0] * x
    for r in range(1, NP):
        acc = acc + table[r] * pltpu.roll(x, r, 0)
    return acc


def tile(i, j):
    return pl.ds(pl.multiple_of(i * 64 + j * 8, 8), 8)


def face_rows(k, a, end):
    if k == 0:
        return pl.ds(pl.multiple_of(end * 64 + a * 8, 8), 8)
    if k == 1:
        return pl.ds(pl.multiple_of(a * 64 + end * 8, 8), 8)
    return pl.ds(a * 64 + end, 8, stride=8)


def grid_rows(a):
    return pl.ds(pl.multiple_of(a * 8, 8), 8)


def wide(row):
    return jnp.broadcast_to(row, (NP, LANES))


def select_groups(group, pieces):
    out = pieces[-1][1]
    for g, value in pieces[:-1]:
        out = jnp.where(group == g, value, out)
    return out


def primitive(u):
    inv = 1.0 / u[0]
    v = [u[1] * inv, u[2] * inv, u[3] * inv]
    p = (GAMMA - 1.0) * (u[4] - 0.5 * (u[1] * v[0] + u[2] * v[1] + u[3] * v[2]))
    return v, p, p * inv


def orient(load, store, turns, back):
    m = [load(grid_rows(a)) for a in range(NP)]
    t = [load(pl.ds(a, 8, stride=8)) for a in range(NP)]
    row = iota(0)
    one, three = (3, 1) if back else (1, 3)
    kept = (turns == 0) | (turns == one)
    index = jnp.where(kept, row, 7 - row)
    for a in range(NP):
        x = jnp.where(turns == 0, m[a], jnp.where(turns == one, t[7 - a], jnp.where(turns == 2, m[7 - a], t[a])))
        store(a, row_gather(x, index))


def kernel(n_dom, n_sub, state_ref, links_ref, send_ref, upd_out, sec_out,
           st, prim, grad, flux, upd, sec, low, pre, sl, mf, sf, send1, recv1, send2, recv2,
           in_sem, out_sem, send_sem, recv_sem):
    me = {"dom": lax.axis_index("dom"), "sub": lax.axis_index("sub")}
    size = {"dom": n_dom, "sub": n_sub}

    def device(place):
        axis, offset = OFFSETS[place]
        at = dict(me)
        at[axis] = lax.rem(me[axis] + offset + size[axis], size[axis])
        return (at["dom"], at["sub"])

    load_state = pltpu.make_async_copy(state_ref, st, in_sem)
    load_state.start()
    barrier = pltpu.get_barrier_semaphore()
    for place in range(10):
        pl.semaphore_signal(barrier, inc=1, device_id=device(place), device_id_type=pl.DeviceIdType.MESH)

    def remote(phase, place):
        src, dst = (send1, recv1) if phase == 0 else (send2, recv2)
        return pltpu.make_async_remote_copy(
            src_ref=src.at[place],
            dst_ref=dst.at[MIRROR[place]],
            send_sem=send_sem.at[phase, place],
            recv_sem=recv_sem.at[phase, MIRROR[place]],
            device_id=device(place),
            device_id_type=pl.DeviceIdType.MESH,
        )

    lane = iota(1)
    group = lane >> 5
    slot = lane & 31
    place_of = [
        jnp.where(group < 2, 2 * group + 1, 2 * group),
        jnp.where(group < 2, 2 * group, 2 * group + 1),
        8 + (group & 1),
    ]
    table = send_ref[...]
    t0, t1 = wide(table[:, 0:128]), wide(table[:, 128:256])
    t2 = wide(jnp.concatenate([table[:, 256:320], table[:, 256:320]], axis=1))
    send_index = []
    for k in range(2):
        at = (place_of[k] & 3) * 32 + slot
        send_index.append(jnp.where(group < 2, lane_gather(t0, at), lane_gather(t1, at)) & 127)
    send_index.append(t2 & 127)

    partner = [wide(links_ref[0, k : k + 1, :]) for k in range(3)]
    source = [wide(links_ref[1, k : k + 1, :]) for k in range(3)]
    turns = [wide(links_ref[2, k : k + 1, :]) for k in range(3)]

    def received_index(k, value):
        q = value - 384
        if k == 2:
            first = 1 - ((q >> 5) - 8)
        else:
            first = 3 - (q >> 6)
        return [(((first + j) & 3) * 32 + (q & 31)) for j in range(4)]

    return_index = []
    for k in range(3):
        column = jnp.broadcast_to(jnp.transpose(partner[k])[:, 0:1], (LANES, LANES))
        code = jnp.broadcast_to((384 + place_of[k] * 32 + slot)[0:1, :], (LANES, LANES))
        number = lax.broadcasted_iota(jnp.int32, (LANES, LANES), 0).astype(jnp.float32)
        found = jnp.sum(jnp.where(column == code, number, 0.0), axis=0, keepdims=True)
        return_index.append(wide(found.astype(jnp.int32)))

    def pack(k, get, index, buffer):
        rolled = [index] + [pltpu.roll(index, 32 * j, 1) for j in range(1, 4)]
        for r in range(10):
            u = [lane_gather(get(10 * j + r), rolled[j]) for j in range(4)]
            for b, place in enumerate(PLACES[k]):
                buffer[place, r * 8 : r * 8 + 8, :] = select_groups(group, [((b + j) % 4, u[j]) for j in range(4)])

    def unpack(k, r, buffer):
        v = [buffer[place, r * 8 : r * 8 + 8, :] for place in PLACES[k]]
        last = len(v) - 1
        return [select_groups(group, [((last - b + j) % 4, v[b]) for b in range(len(v))]) for j in range(4)]

    load_state.wait()
    for k in range(3):
        for c in range(5):
            for a in range(NP):
                low[k, c, a * 8 : a * 8 + 8, :] = st[c, face_rows(k, a, 0), :]
        pack(k, lambda n: low[k, n // 8, (n % 8) * 8 : (n % 8) * 8 + 8, :], send_index[k], send1)

    pl.semaphore_wait(barrier, 10)
    order = [0, 7, 1, 6, 2, 5, 3, 4, 8, 9]
    first = [remote(0, place) for place in order]
    for copy in first:
        copy.start()

    def prim_body(t, carry):
        rows = pl.ds(pl.multiple_of(t * 8, 8), 8)
        u = [st[c, rows, :] for c in range(5)]
        v, p, theta = primitive(u)
        for a in range(3):
            prim[a, rows, :] = v[a]
        prim[3, rows, :] = theta
        return carry

    lax.fori_loop(0, 64, prim_body, 0, unroll=4)

    grad_rows = roll_table(GRAD_MAT)

    def grad_body(s, carry):
        for a in range(4):
            xs = [prim[a, tile(i, s), :] for i in range(NP)]
            for i, y in enumerate(pencil(GRAD_MAT, xs)):
                grad[a, tile(i, s), :] = y
            xs = [prim[a, tile(s, j), :] for j in range(NP)]
            for j, y in enumerate(pencil(GRAD_MAT, xs)):
                grad[4 + a, tile(s, j), :] = y
            for j in range(NP):
                grad[8 + a, tile(s, j), :] = along_rows(grad_rows, xs[j])
        return carry

    lax.fori_loop(0, NP, grad_body, 0)

    for place in order:
        copy = remote(0, MIRROR[place])
        copy.wait_recv()
    for k in range(3):
        index = received_index(k, partner[k])
        own = partner[k] & 127
        local = partner[k] < 384
        for r in range(10):
            u = unpack(k, r, recv1)
            for j in range(4):
                n = 10 * j + r
                rows = slice((n % 8) * 8, (n % 8) * 8 + 8)
                pre[n // 8, rows, :] = jnp.where(
                    local, lane_gather(low[k, n // 8, rows, :], own), lane_gather(u[j], index[j])
                )
        for c in range(5):
            def keep(a, value, k=k, c=c):
                sl[k, c, a * 8 : a * 8 + 8, :] = value
            orient(lambda rows: pre[c, rows, :], keep, turns[k], False)

        def slave_body(a, carry, k=k):
            rows, at = grid_rows(a), face_rows(k, a, 7)
            s = [sl[k, c, rows, :] for c in range(5)]
            u = [st[c, at, :] for c in range(5)]
            vs, ps, ths = primitive(s)
            v = [prim[c, at, :] for c in range(3)]
            th = prim[3, at, :]
            p = th * u[0]
            for c in range(4):
                jump = (vs + [ths])[c] - (v + [th])[c]
                grad[4 * k + c, at, :] = grad[4 * k + c, at, :] + LIFT * jump
            speed = jnp.maximum(jnp.abs(v[k]) + jnp.sqrt(GAMMA * th), jnp.abs(vs[k]) + jnp.sqrt(GAMMA * ths))
            weight = 0.5 * speed + PENALTY
            e = [u[1 + k]] + [u[1 + j] * v[k] for j in range(3)] + [(u[4] + p) * v[k]]
            es = [s[1 + k]] + [s[1 + j] * vs[k] for j in range(3)] + [(s[4] + ps) * vs[k]]
            e[1 + k] = e[1 + k] + p
            es[1 + k] = es[1 + k] + ps
            for c in range(5):
                mf[k, c, rows, :] = 0.5 * (e[c] + es[c]) + weight * (u[c] - s[c])
            return carry

        lax.fori_loop(0, NP, slave_body, 0, unroll=2)

    def stress_heat(k, at, v):
        g = [[grad[4 * d + c, at, :] for c in range(3)] for d in range(3)]
        div = (2.0 / 3.0) * (g[0][0] + g[1][1] + g[2][2])
        stress = [g[k][j] + g[j][k] for j in range(3)]
        stress[k] = stress[k] - div
        heat = stress[0] * v[0] + stress[1] * v[1] + stress[2] * v[2]
        return stress, heat + (CONDUCTION / VISCOSITY) * grad[4 * k + 3, at, :]

    for k in (1, 0, 2):
        def viscous_body(a, carry, k=k):
            rows, at = grid_rows(a), face_rows(k, a, 7)
            v = [prim[c, at, :] for c in range(3)]
            stress, heat = stress_heat(k, at, v)
            for j in range(3):
                mf[k, 1 + j, rows, :] = mf[k, 1 + j, rows, :] - stress[j]
            mf[k, 4, rows, :] = mf[k, 4, rows, :] - heat
            return carry

        lax.fori_loop(0, NP, viscous_body, 0, unroll=2)
        for c in range(5):
            def keep(a, value, k=k, c=c):
                sf[k, c, a * 8 : a * 8 + 8, :] = value
            orient(lambda rows: mf[k, c, rows, :], keep, turns[k], True)
        pack(k, lambda n: sf[k, n // 8, (n % 8) * 8 : (n % 8) * 8 + 8, :], return_index[k], send2)
        for place in PLACES[k]:
            remote(1, place).start()

    def flux_body(t, carry):
        rows = pl.ds(pl.multiple_of(t * 8, 8), 8)
        u = [st[c, rows, :] for c in range(5)]
        v = [prim[c, rows, :] for c in range(3)]
        p = prim[3, rows, :] * u[0]
        g = [[grad[4 * d + c, rows, :] for c in range(4)] for d in range(3)]
        div = (2.0 / 3.0) * (g[0][0] + g[1][1] + g[2][2])
        stress = {}
        number = 0
        for a in range(3):
            for b in range(a, 3):
                stress[a, b] = stress[b, a] = g[a][b] + g[b][a] if a != b else 2.0 * g[a][a] - div
                total = u[1 + a] * v[b] - stress[a, b]
                flux[number, rows, :] = total + p if a == b else total
                number += 1
        enthalpy = u[4] + p
        for k in range(3):
            heat = stress[k, 0] * v[0] + stress[k, 1] * v[1] + stress[k, 2] * v[2]
            heat = heat + (CONDUCTION / VISCOSITY) * g[k][3]
            flux[6 + k, rows, :] = enthalpy * v[k] - heat
        return carry

    lax.fori_loop(0, 64, flux_body, 0, unroll=2)

    flux_rows = roll_table(FLUX_MAT)
    pairs = {(0, 0): 0, (0, 1): 1, (0, 2): 2, (1, 1): 3, (1, 2): 4, (2, 2): 5}

    def flux_of(k, c, rows):
        if c == 0:
            return st[1 + k, rows, :]
        if c == 4:
            return flux[6 + k, rows, :]
        return flux[pairs[min(k, c - 1), max(k, c - 1)], rows, :]

    def first_body(s, carry):
        for c in range(5):
            xs = [flux_of(0, c, tile(i, s)) for i in range(NP)]
            for i, y in enumerate(pencil(FLUX_MAT, xs)):
                upd[c, tile(i, s), :] = y
        return carry

    lax.fori_loop(0, NP, first_body, 0)

    def other_body(s, carry):
        for c in range(5):
            ys = pencil(FLUX_MAT, [flux_of(1, c, tile(s, j)) for j in range(NP)])
            for j in range(NP):
                rows = tile(s, j)
                upd[c, rows, :] = upd[c, rows, :] + ys[j] + along_rows(flux_rows, flux_of(2, c, rows))
        return carry

    lax.fori_loop(0, NP, other_body, 0)

    for k in range(3):
        for c in range(5):
            for a in range(NP):
                at = face_rows(k, a, 7)
                upd[c, at, :] = upd[c, at, :] - FACE_SCALE * mf[k, c, a * 8 : a * 8 + 8, :]

    for place in order:
        remote(1, MIRROR[place]).wait_recv()
    for k in range(3):
        index = received_index(k, source[k])
        own = source[k] & 127
        local = source[k] < 384
        for r in range(10):
            u = unpack(k, r, recv2)
            for j in range(4):
                n = 10 * j + r
                c, a = n // 8, n % 8
                value = jnp.where(
                    local, lane_gather(sf[k, c, a * 8 : a * 8 + 8, :], own), lane_gather(u[j], index[j])
                )
                at = face_rows(k, a, 0)
                upd[c, at, :] = upd[c, at, :] + FACE_SCALE * value

    def section_body(t, carry):
        rows = pl.ds(pl.multiple_of(t * 8, 8), 8)
        for c in range(5):
            sec[c, rows, :] = st[c, rows, :] + SECTION_WEIGHT * upd[c, rows, :]
        return carry

    store_upd = pltpu.make_async_copy(upd, upd_out, out_sem.at[0])
    store_upd.start()
    lax.fori_loop(0, 64, section_body, 0, unroll=4)
    store_sec = pltpu.make_async_copy(sec, sec_out, out_sem.at[1])
    store_sec.start()
    for phase in range(2):
        for place in order:
            remote(phase, place).wait_send()
    store_upd.wait()
    store_sec.wait()


def per_device(n_dom, n_sub, state, face_links, send_from):
    whole = pltpu.VMEM
    f32 = jnp.float32
    field = (512, LANES)
    return pl.pallas_call(
        functools.partial(kernel, n_dom, n_sub),
        out_shape=(jax.ShapeDtypeStruct(state.shape, f32), jax.ShapeDtypeStruct(state.shape, f32)),
        in_specs=[
            pl.BlockSpec(memory_space=pl.ANY),
            pl.BlockSpec(memory_space=whole),
            pl.BlockSpec(memory_space=whole),
        ],
        out_specs=(pl.BlockSpec(memory_space=pl.ANY), pl.BlockSpec(memory_space=pl.ANY)),
        scratch_shapes=[
            whole((5,) + field, f32),
            whole((4,) + field, f32),
            whole((12,) + field, f32),
            whole((9,) + field, f32),
            whole((5,) + field, f32),
            whole((5,) + field, f32),
            whole((3, 5, 64, LANES), f32),
            whole((5, 64, LANES), f32),
            whole((3, 5, 64, LANES), f32),
            whole((3, 5, 64, LANES), f32),
            whole((3, 5, 64, LANES), f32),
            whole((10, 80, LANES), f32),
            whole((10, 80, LANES), f32),
            whole((10, 80, LANES), f32),
            whole((10, 80, LANES), f32),
            pltpu.SemaphoreType.DMA,
            pltpu.SemaphoreType.DMA((2,)),
            pltpu.SemaphoreType.DMA((2, 10)),
            pltpu.SemaphoreType.DMA((2, 10)),
        ],
        compiler_params=pltpu.CompilerParams(
            collective_id=0, has_side_effects=True, vmem_limit_bytes=48 * 1024 * 1024
        ),
        name="section",
    )(state, face_links, send_from)


def solution(mesh):
    in_specs = (
        P(None, None, ("dom", "sub")),
        P(None, None, ("dom", "sub")),
        P(("dom", "sub"), None),
    )
    out_specs = (P(None, None, ("dom", "sub")), P(None, None, ("dom", "sub")))
    return jax.shard_map(
        functools.partial(per_device, mesh.shape["dom"], mesh.shape["sub"]),
        mesh=mesh, in_specs=in_specs, out_specs=out_specs, check_vma=False
    )
```

time: 249 us -> 34.7 us (0.14)
  the two profiles are of different devices: /device:TPU:56 before, /device:TPU:1 now
where the time goes in v1:
time: 34.7 us; the launch traced here: 34.5 us
  Pallas kernels  29 us (84%)
  local copies, waits for them, and re-layouts  4.8 us (14%)
  between operations  0.65 us (2%)
    pallas_call x1, Pallas kernels, per_device(): pl.pallas_call(functools.partial(kernel, n_dom, n_sub), out_shape=(jax.Sh...  29 us
    unnamed x8, local copies, waits for them, and re-layouts  4.8 us

profile of v1, /device:TPU:1, one launch (start us, length us, event | category | flops | bytes accessed | tf_op | source)
XLA Modules:
  0.0 34.5 jit_solution(15605759102500136888)
XLA Ops:
  0.6 0.0 copy-start
  0.6 1.3 %copy-done = f32[5,512,128]{2,1,0:T(8,128)S(1)} copy-done((f32[5,512,128]{2,1,0:T(8,128)S(1)}, f32[5,512,128]{2,1,0:T(8,128)}, u32[]{:S(2)}) %copy-start) | copy-done | bytes 1310744
  1.9 0.0 copy-start.1
  1.9 0.7 %copy-done.1 = s32[3,3,128]{2,1,0:T(4,128)S(1)} copy-done((s32[3,3,128]{2,1,0:T(4,128)S(1)}, s32[3,3,128]{2,1,0:T(4,128)}, u32[]{:S(2)}) %copy-start.1) | copy-done | bytes 4632
  2.6 0.0 copy-start.2
  2.6 0.7 %copy-done.2 = s32[1,320]{1,0:T(1,128)S(1)} copy-done((s32[1,320]{1,0:T(1,128)S(1)}, s32[1,320]{1,0:T(1,128)}, u32[]{:S(2)}) %copy-start.2) | copy-done | bytes 1304
  3.3 29.0 %section.1 = (f32[5,512,128]{2,1,0:T(8,128)S(1)}, f32[5,512,128]{2,1,0:T(8,128)S(1)}) custom-call(f32[5,512,128]{2,1,0:T(8,128)S(1)} %copy-done, s32[3,3,128]{2,1,0:T(4,128)S(1)} %copy-done.1, s32[1,320]{1,0:T(1,128)S(1)} %copy-done.2), custom_call_target="tpu_custom_call" | custom-call | tf_op jit(solution)/shard_map/section/pallas_call | solution.py:432
  32.4 1.1 %copy.7 = f32[5,512,128]{2,1,0:T(8,128)} copy(f32[5,512,128]{2,1,0:T(8,128)S(1)} %get-tuple-element.4) | data formatting | bytes 2621440
  33.4 1.1 %copy.8 = f32[5,512,128]{2,1,0:T(8,128)} copy(f32[5,512,128]{2,1,0:T(8,128)S(1)} %get-tuple-element.5) | data formatting | bytes 2621440
Async XLA Ops:
  0.6 1.3 %copy-start = (f32[5,512,128]{2,1,0:T(8,128)S(1)}, f32[5,512,128]{2,1,0:T(8,128)}, u32[]{:S(2)}) copy-start(f32[5,512,128]{2,1,0:T(8,128)} %state_ref.1) | copy-start | bytes 3932164
  1.9 0.7 %copy-start.1 = (s32[3,3,128]{2,1,0:T(4,128)S(1)}, s32[3,3,128]{2,1,0:T(4,128)}, u32[]{:S(2)}) copy-start(s32[3,3,128]{2,1,0:T(4,128)} %links_ref.1) | copy-start | bytes 13828
  2.6 0.7 %copy-start.2 = (s32[1,320]{1,0:T(1,128)S(1)}, s32[1,320]{1,0:T(1,128)}, u32[]{:S(2)}) copy-start(s32[1,320]{1,0:T(1,128)} %send_ref.1) | copy-start | bytes 3844

commit v2 on v1

--- a/solution.py
+++ b/solution.py
@@ -143,9 +143,9 @@
         store(a, row_gather(x, index))
 
 
-def kernel(n_dom, n_sub, state_ref, links_ref, send_ref, upd_out, sec_out,
-           st, prim, grad, flux, upd, sec, low, pre, sl, mf, sf, send1, recv1, send2, recv2,
-           in_sem, out_sem, send_sem, recv_sem):
+def kernel(n_dom, n_sub, state_hbm, links_hbm, send_hbm, upd, st,
+           links_ref, send_ref, prim, grad, flux, low, pre, sl, mf, sf, send1, recv1, send2, recv2,
+           in_sem, send_sem, recv_sem):
     me = {"dom": lax.axis_index("dom"), "sub": lax.axis_index("sub")}
     size = {"dom": n_dom, "sub": n_sub}
 
@@ -155,11 +155,15 @@
         at[axis] = lax.rem(me[axis] + offset + size[axis], size[axis])
         return (at["dom"], at["sub"])
 
-    load_state = pltpu.make_async_copy(state_ref, st, in_sem)
-    load_state.start()
+    loads = [pltpu.make_async_copy(state_hbm.at[c], st.at[c], in_sem.at[c]) for c in range(5)]
+    loads.append(pltpu.make_async_copy(links_hbm, links_ref, in_sem.at[5]))
+    loads.append(pltpu.make_async_copy(send_hbm, send_ref, in_sem.at[6]))
     barrier = pltpu.get_barrier_semaphore()
     for place in range(10):
         pl.semaphore_signal(barrier, inc=1, device_id=device(place), device_id_type=pl.DeviceIdType.MESH)
+
+    for load in loads[::-1]:
+        load.start()
 
     def remote(phase, place):
         src, dst = (send1, recv1) if phase == 0 else (send2, recv2)
@@ -172,6 +176,8 @@
             device_id_type=pl.DeviceIdType.MESH,
         )
 
+    loads[6].wait()
+    loads[5].wait()
     lane = iota(1)
     group = lane >> 5
     slot = lane & 31
@@ -212,7 +218,7 @@
     def pack(k, get, index, buffer):
         rolled = [index] + [pltpu.roll(index, 32 * j, 1) for j in range(1, 4)]
         for r in range(10):
-            u = [lane_gather(get(10 * j + r), rolled[j]) for j in range(4)]
+            u = [lane_gather(get(4 * r + j), rolled[j]) for j in range(4)]
             for b, place in enumerate(PLACES[k]):
                 buffer[place, r * 8 : r * 8 + 8, :] = select_groups(group, [((b + j) % 4, u[j]) for j in range(4)])
 
@@ -221,7 +227,8 @@
         last = len(v) - 1
         return [select_groups(group, [((last - b + j) % 4, v[b]) for b in range(len(v))]) for j in range(4)]
 
-    load_state.wait()
+    for c in range(5):
+        loads[c].wait()
     for k in range(3):
         for c in range(5):
             for a in range(NP):
@@ -271,7 +278,7 @@
         for r in range(10):
             u = unpack(k, r, recv1)
             for j in range(4):
-                n = 10 * j + r
+                n = 4 * r + j
                 rows = slice((n % 8) * 8, (n % 8) * 8 + 8)
                 pre[n // 8, rows, :] = jnp.where(
                     local, lane_gather(low[k, n // 8, rows, :], own), lane_gather(u[j], index[j])
@@ -399,7 +406,7 @@
         for r in range(10):
             u = unpack(k, r, recv2)
             for j in range(4):
-                n = 10 * j + r
+                n = 4 * r + j
                 c, a = n // 8, n % 8
                 value = jnp.where(
                     local, lane_gather(sf[k, c, a * 8 : a * 8 + 8, :], own), lane_gather(u[j], index[j])
@@ -407,44 +414,45 @@
                 at = face_rows(k, a, 0)
                 upd[c, at, :] = upd[c, at, :] + FACE_SCALE * value
 
-    def section_body(t, carry):
-        rows = pl.ds(pl.multiple_of(t * 8, 8), 8)
-        for c in range(5):
-            sec[c, rows, :] = st[c, rows, :] + SECTION_WEIGHT * upd[c, rows, :]
-        return carry
-
-    store_upd = pltpu.make_async_copy(upd, upd_out, out_sem.at[0])
-    store_upd.start()
-    lax.fori_loop(0, 64, section_body, 0, unroll=4)
-    store_sec = pltpu.make_async_copy(sec, sec_out, out_sem.at[1])
-    store_sec.start()
     for phase in range(2):
         for place in order:
             remote(phase, place).wait_send()
-    store_upd.wait()
-    store_sec.wait()
+
+
+def writer(upd, st, upd_out, sec_out, sec, sem):
+    copies = []
+    for c in range(5):
+        copies.append(pltpu.make_async_copy(upd.at[c], upd_out.at[c], sem.at[0, c]))
+        copies[-1].start()
+    for c in range(5):
+        sec[c] = st[c] + SECTION_WEIGHT * upd[c]
+        copies.append(pltpu.make_async_copy(sec.at[c], sec_out.at[c], sem.at[1, c]))
+        copies[-1].start()
+    for copy in copies:
+        copy.wait()
 
 
 def per_device(n_dom, n_sub, state, face_links, send_from):
     whole = pltpu.VMEM
     f32 = jnp.float32
     field = (512, LANES)
-    return pl.pallas_call(
+    hbm = pl.BlockSpec(memory_space=pltpu.HBM)
+    inside = pl.BlockSpec(memory_space=whole)
+    like = jax.ShapeDtypeStruct(state.shape, f32)
+    state, face_links, send_from = [
+        pltpu.with_memory_space_constraint(x, pltpu.HBM) for x in (state, face_links, send_from)
+    ]
+    upd, st = pl.pallas_call(
         functools.partial(kernel, n_dom, n_sub),
-        out_shape=(jax.ShapeDtypeStruct(state.shape, f32), jax.ShapeDtypeStruct(state.shape, f32)),
-        in_specs=[
-            pl.BlockSpec(memory_space=pl.ANY),
-            pl.BlockSpec(memory_space=whole),
-            pl.BlockSpec(memory_space=whole),
-        ],
-        out_specs=(pl.BlockSpec(memory_space=pl.ANY), pl.BlockSpec(memory_space=pl.ANY)),
+        out_shape=(like, like),
+        in_specs=[hbm, hbm, hbm],
+        out_specs=(inside, inside),
         scratch_shapes=[
-            whole((5,) + field, f32),
+            whole(face_links.shape, jnp.int32),
+            whole(send_from.shape, jnp.int32),
             whole((4,) + field, f32),
             whole((12,) + field, f32),
             whole((9,) + field, f32),
-            whole((5,) + field, f32),
-            whole((5,) + field, f32),
             whole((3, 5, 64, LANES), f32),
             whole((5, 64, LANES), f32),
             whole((3, 5, 64, LANES), f32),
@@ -454,16 +462,24 @@
             whole((10, 80, LANES), f32),
             whole((10, 80, LANES), f32),
             whole((10, 80, LANES), f32),
-            pltpu.SemaphoreType.DMA,
-            pltpu.SemaphoreType.DMA((2,)),
+            pltpu.SemaphoreType.DMA((7,)),
             pltpu.SemaphoreType.DMA((2, 10)),
             pltpu.SemaphoreType.DMA((2, 10)),
         ],
         compiler_params=pltpu.CompilerParams(
-            collective_id=0, has_side_effects=True, vmem_limit_bytes=48 * 1024 * 1024
+            collective_id=0, has_side_effects=True, vmem_limit_bytes=40 * 1024 * 1024
         ),
+        name="rate",
+    )(state, face_links, send_from)
+    return pl.pallas_call(
+        writer,
+        out_shape=(like, like),
+        in_specs=[inside, inside],
+        out_specs=(hbm, hbm),
+        scratch_shapes=[whole((5,) + field, f32), pltpu.SemaphoreType.DMA((2, 5))],
+        compiler_params=pltpu.CompilerParams(vmem_limit_bytes=16 * 1024 * 1024),
         name="section",
-    )(state, face_links, send_from)
+    )(upd, st)
 
 
 def solution(mesh):

time: 34.7 us -> 30.9 us (0.89)
  local copies, waits for them, and re-layouts: 4.8 us -> 0 us
  Pallas kernels: 29 us -> 30.1 us
    unnamed x8 -> x0, local copies, waits for them, and re-layouts: 4.8 us -> none
    pallas_call x1 -> x2, Pallas kernels: 29 us -> 30.1 us  [the longest x1 28.5 us: per_device(): pl.pallas_call(functools.partial(kernel, n_dom, n_sub), out_shape=(like,...]
where the time goes in v2:
time: 30.9 us; the launch traced here: 30.7 us
  Pallas kernels  30.1 us (97%)
  between operations  0.64 us (2%)
    pallas_call x1, Pallas kernels, per_device(): pl.pallas_call(functools.partial(kernel, n_dom, n_sub), out_shape=(like,...  28.5 us
    pallas_call x1, Pallas kernels, per_device(): pl.pallas_call(writer, out_shape=(like, like), in_specs=[inside, inside],...  1.57 us

profile of v2, /device:TPU:1, one launch (start us, length us, event | category | flops | bytes accessed | tf_op | source)
XLA Modules:
  0.0 30.7 jit_solution(10623803976989065633)
XLA Ops:
  0.6 28.5 %rate.1 = (f32[5,512,128]{2,1,0:T(8,128)S(1)}, f32[5,512,128]{2,1,0:T(8,128)S(1)}) custom-call(f32[5,512,128]{2,1,0:T(8,128)} %state_hbm.1, s32[3,3,128]{2,1,0:T(4,128)} %links_hbm.1, s32[1,320]{1,0:T(1,128)} %send_hbm.1), custom_call_target="tpu_custom_call" | custom-call | tf_op jit(solution)/shard_map/rate/pallas_call | solution.py:445
  29.2 1.6 %section.1 = (f32[5,512,128]{2,1,0:T(8,128)}, f32[5,512,128]{2,1,0:T(8,128)}) custom-call(f32[5,512,128]{2,1,0:T(8,128)S(1)} %get-tuple-element.4.upd, f32[5,512,128]{2,1,0:T(8,128)S(1)} %get-tuple-element.5.st), custom_call_target="tpu_custom_call" | custom-call | tf_op jit(solution)/shard_map/section/pallas_call | solution.py:474

commit v3 on v2

--- a/solution.py
+++ b/solution.py
@@ -155,12 +155,22 @@
         at[axis] = lax.rem(me[axis] + offset + size[axis], size[axis])
         return (at["dom"], at["sub"])
 
+    def exists(place):
+        axis, offset = OFFSETS[place]
+        return (me[axis] + offset >= 0) & (me[axis] + offset < size[axis])
+
     loads = [pltpu.make_async_copy(state_hbm.at[c], st.at[c], in_sem.at[c]) for c in range(5)]
     loads.append(pltpu.make_async_copy(links_hbm, links_ref, in_sem.at[5]))
     loads.append(pltpu.make_async_copy(send_hbm, send_ref, in_sem.at[6]))
     barrier = pltpu.get_barrier_semaphore()
+    neighbours = 0
     for place in range(10):
-        pl.semaphore_signal(barrier, inc=1, device_id=device(place), device_id_type=pl.DeviceIdType.MESH)
+        neighbours = neighbours + exists(place).astype(jnp.int32)
+
+        @pl.when(exists(place))
+        def _(place=place):
+            pl.semaphore_signal(barrier, inc=1, device_id=device(place), device_id_type=pl.DeviceIdType.MESH)
+
 
     for load in loads[::-1]:
         load.start()
@@ -175,6 +185,21 @@
             device_id=device(place),
             device_id_type=pl.DeviceIdType.MESH,
         )
+
+    def start(phase, place):
+        @pl.when(exists(place))
+        def _():
+            remote(phase, place).start()
+
+    def wait_recv(phase, place):
+        @pl.when(exists(place))
+        def _():
+            remote(phase, MIRROR[place]).wait_recv()
+
+    def wait_send(phase, place):
+        @pl.when(exists(place))
+        def _():
+            remote(phase, place).wait_send()
 
     loads[6].wait()
     loads[5].wait()
@@ -235,11 +260,10 @@
                 low[k, c, a * 8 : a * 8 + 8, :] = st[c, face_rows(k, a, 0), :]
         pack(k, lambda n: low[k, n // 8, (n % 8) * 8 : (n % 8) * 8 + 8, :], send_index[k], send1)
 
-    pl.semaphore_wait(barrier, 10)
+    pl.semaphore_wait(barrier, neighbours)
     order = [0, 7, 1, 6, 2, 5, 3, 4, 8, 9]
-    first = [remote(0, place) for place in order]
-    for copy in first:
-        copy.start()
+    for place in order:
+        start(0, place)
 
     def prim_body(t, carry):
         rows = pl.ds(pl.multiple_of(t * 8, 8), 8)
@@ -268,10 +292,9 @@
 
     lax.fori_loop(0, NP, grad_body, 0)
 
-    for place in order:
-        copy = remote(0, MIRROR[place])
-        copy.wait_recv()
-    for k in range(3):
+    for k in (2, 1, 0):
+        for place in PLACES[k]:
+            wait_recv(0, place)
         index = received_index(k, partner[k])
         own = partner[k] & 127
         local = partner[k] < 384
@@ -309,7 +332,7 @@
                 mf[k, c, rows, :] = 0.5 * (e[c] + es[c]) + weight * (u[c] - s[c])
             return carry
 
-        lax.fori_loop(0, NP, slave_body, 0, unroll=2)
+        lax.fori_loop(0, NP, slave_body, 0, unroll=8)
 
     def stress_heat(k, at, v):
         g = [[grad[4 * d + c, at, :] for c in range(3)] for d in range(3)]
@@ -329,14 +352,14 @@
             mf[k, 4, rows, :] = mf[k, 4, rows, :] - heat
             return carry
 
-        lax.fori_loop(0, NP, viscous_body, 0, unroll=2)
+        lax.fori_loop(0, NP, viscous_body, 0, unroll=8)
         for c in range(5):
             def keep(a, value, k=k, c=c):
                 sf[k, c, a * 8 : a * 8 + 8, :] = value
             orient(lambda rows: mf[k, c, rows, :], keep, turns[k], True)
         pack(k, lambda n: sf[k, n // 8, (n % 8) * 8 : (n % 8) * 8 + 8, :], return_index[k], send2)
         for place in PLACES[k]:
-            remote(1, place).start()
+            start(1, place)
 
     def flux_body(t, carry):
         rows = pl.ds(pl.multiple_of(t * 8, 8), 8)
@@ -397,9 +420,9 @@
                 at = face_rows(k, a, 7)
                 upd[c, at, :] = upd[c, at, :] - FACE_SCALE * mf[k, c, a * 8 : a * 8 + 8, :]
 
-    for place in order:
-        remote(1, MIRROR[place]).wait_recv()
-    for k in range(3):
+    for k in (2, 1, 0):
+        for place in PLACES[k]:
+            wait_recv(1, place)
         index = received_index(k, source[k])
         own = source[k] & 127
         local = source[k] < 384
@@ -416,7 +439,7 @@
 
     for phase in range(2):
         for place in order:
-            remote(phase, place).wait_send()
+            wait_send(phase, place)
 
 
 def writer(upd, st, upd_out, sec_out, sec, sem):

time: 30.9 us -> 22.1 us (0.72)
  Pallas kernels: 30.1 us -> 21.3 us
    pallas_call x1, Pallas kernels: 28.5 us -> 19.7 us  [per_device(): pl.pallas_call(functools.partial(kernel, n_dom, n_sub), out_shape=(like,...]
where the time goes in v3:
time: 22.1 us; the launch traced here: 21.9 us
  Pallas kernels  21.3 us (96%)
  between operations  0.64 us (3%)
    pallas_call x1, Pallas kernels, per_device(): pl.pallas_call(functools.partial(kernel, n_dom, n_sub), out_shape=(like,...  19.7 us
    pallas_call x1, Pallas kernels, per_device(): pl.pallas_call(writer, out_shape=(like, like), in_specs=[inside, inside],...  1.57 us

profile of v3, /device:TPU:1, one launch (start us, length us, event | category | flops | bytes accessed | tf_op | source)
XLA Modules:
  0.0 21.9 jit_solution(9478842133529697354)
XLA Ops:
  0.6 19.7 %rate.1 = (f32[5,512,128]{2,1,0:T(8,128)S(1)}, f32[5,512,128]{2,1,0:T(8,128)S(1)}) custom-call(f32[5,512,128]{2,1,0:T(8,128)} %state_hbm.1, s32[3,3,128]{2,1,0:T(4,128)} %links_hbm.1, s32[1,320]{1,0:T(1,128)} %send_hbm.1), custom_call_target="tpu_custom_call" | custom-call | tf_op jit(solution)/shard_map/rate/pallas_call | solution.py:468
  20.4 1.6 %section.1 = (f32[5,512,128]{2,1,0:T(8,128)}, f32[5,512,128]{2,1,0:T(8,128)}) custom-call(f32[5,512,128]{2,1,0:T(8,128)S(1)} %get-tuple-element.4.upd, f32[5,512,128]{2,1,0:T(8,128)S(1)} %get-tuple-element.5.st), custom_call_target="tpu_custom_call" | custom-call | tf_op jit(solution)/shard_map/section/pallas_call | solution.py:497

commit v4 on v3

--- a/solution.py
+++ b/solution.py
@@ -152,7 +152,7 @@
     def device(place):
         axis, offset = OFFSETS[place]
         at = dict(me)
-        at[axis] = lax.rem(me[axis] + offset + size[axis], size[axis])
+        at[axis] = me[axis] + offset
         return (at["dom"], at["sub"])
 
     def exists(place):
@@ -186,6 +186,17 @@
             device_id_type=pl.DeviceIdType.MESH,
         )
 
+    def arriving(phase, place):
+        src, dst = (send1, recv1) if phase == 0 else (send2, recv2)
+        return pltpu.make_async_remote_copy(
+            src_ref=src.at[place],
+            dst_ref=dst.at[place],
+            send_sem=send_sem.at[phase, place],
+            recv_sem=recv_sem.at[phase, place],
+            device_id=device(place),
+            device_id_type=pl.DeviceIdType.MESH,
+        )
+
     def start(phase, place):
         @pl.when(exists(place))
         def _():
@@ -194,7 +205,7 @@
     def wait_recv(phase, place):
         @pl.when(exists(place))
         def _():
-            remote(phase, MIRROR[place]).wait_recv()
+            arriving(phase, place).wait_recv()
 
     def wait_send(phase, place):
         @pl.when(exists(place))

time: 22.1 us -> 22.1 us (level)
  no operation moved by 1% of the time
where the time goes in v4:
time: 22.1 us; the launch traced here: 21.9 us
  Pallas kernels  21.3 us (96%)
  between operations  0.64 us (3%)
    pallas_call x1, Pallas kernels, per_device(): pl.pallas_call(functools.partial(kernel, n_dom, n_sub), out_shape=(like,...  19.7 us
    pallas_call x1, Pallas kernels, per_device(): pl.pallas_call(writer, out_shape=(like, like), in_specs=[inside, inside],...  1.57 us

profile of v4, /device:TPU:1, one launch (start us, length us, event | category | flops | bytes accessed | tf_op | source)
XLA Modules:
  0.0 21.9 jit_solution(13009599855399812682)
XLA Ops:
  0.6 19.7 %rate.1 = (f32[5,512,128]{2,1,0:T(8,128)S(1)}, f32[5,512,128]{2,1,0:T(8,128)S(1)}) custom-call(f32[5,512,128]{2,1,0:T(8,128)} %state_hbm.1, s32[3,3,128]{2,1,0:T(4,128)} %links_hbm.1, s32[1,320]{1,0:T(1,128)} %send_hbm.1), custom_call_target="tpu_custom_call" | custom-call | tf_op jit(solution)/shard_map/rate/pallas_call | solution.py:479
  20.4 1.6 %section.1 = (f32[5,512,128]{2,1,0:T(8,128)}, f32[5,512,128]{2,1,0:T(8,128)}) custom-call(f32[5,512,128]{2,1,0:T(8,128)S(1)} %get-tuple-element.4.upd, f32[5,512,128]{2,1,0:T(8,128)S(1)} %get-tuple-element.5.st), custom_call_target="tpu_custom_call" | custom-call | tf_op jit(solution)/shard_map/section/pallas_call | solution.py:508

commit v5 on v4

--- a/solution.py
+++ b/solution.py
@@ -19,6 +19,7 @@
 OFFSETS = [("dom", o) for o in (-4, -3, -2, -1, 1, 2, 3, 4)] + [("sub", -1), ("sub", 1)]
 MIRROR = [7, 6, 5, 4, 3, 2, 1, 0, 9, 8]
 PLACES = [[1, 3, 4, 6], [0, 2, 5, 7], [8, 9]]
+SENDS = [[1, 6, 3, 4], [0, 7, 2, 5], [8, 9]]
 
 
 def lobatto(points):
@@ -369,7 +370,7 @@
                 sf[k, c, a * 8 : a * 8 + 8, :] = value
             orient(lambda rows: mf[k, c, rows, :], keep, turns[k], True)
         pack(k, lambda n: sf[k, n // 8, (n % 8) * 8 : (n % 8) * 8 + 8, :], return_index[k], send2)
-        for place in PLACES[k]:
+        for place in SENDS[k]:
             start(1, place)
 
     def flux_body(t, carry):

time: 22.1 us -> 22.1 us (level)
  no operation moved by 1% of the time
where the time goes in v5:
time: 22.1 us; the launch traced here: 21.9 us
  Pallas kernels  21.3 us (96%)
  between operations  0.64 us (3%)
    pallas_call x1, Pallas kernels, per_device(): pl.pallas_call(functools.partial(kernel, n_dom, n_sub), out_shape=(like,...  19.7 us
    pallas_call x1, Pallas kernels, per_device(): pl.pallas_call(writer, out_shape=(like, like), in_specs=[inside, inside],...  1.57 us

profile of v5, /device:TPU:1, one launch (start us, length us, event | category | flops | bytes accessed | tf_op | source)
XLA Modules:
  0.0 21.9 jit_solution(5819700369611452927)
XLA Ops:
  0.6 19.7 %rate.1 = (f32[5,512,128]{2,1,0:T(8,128)S(1)}, f32[5,512,128]{2,1,0:T(8,128)S(1)}) custom-call(f32[5,512,128]{2,1,0:T(8,128)} %state_hbm.1, s32[3,3,128]{2,1,0:T(4,128)} %links_hbm.1, s32[1,320]{1,0:T(1,128)} %send_hbm.1), custom_call_target="tpu_custom_call" | custom-call | tf_op jit(solution)/shard_map/rate/pallas_call | solution.py:480
  20.4 1.6 %section.1 = (f32[5,512,128]{2,1,0:T(8,128)}, f32[5,512,128]{2,1,0:T(8,128)}) custom-call(f32[5,512,128]{2,1,0:T(8,128)S(1)} %get-tuple-element.4.upd, f32[5,512,128]{2,1,0:T(8,128)S(1)} %get-tuple-element.5.st), custom_call_target="tpu_custom_call" | custom-call | tf_op jit(solution)/shard_map/section/pallas_call | solution.py:509
